TPU v7x, 32 devices: a whole 2x2x4 slice. The times are simulated.
32 devices in a mesh: dp: 16 (over z, y, core), tensor: 2 (over x).
Axes of the slice: x: 2, y: 2, z: 4, core: 2. Of those that a mesh axis runs over, the one named last changes fastest.
Arguments:
- tokens: bfloat16 [6144, 4096], P(('dp', 'tensor')), may hold values from -21 to 21
- wq_codes: bfloat16 [4096, 1024], P('dp', 'tensor'), may hold values from -4 to 4
- wq_scales: float32 [32, 8], replicated, may hold values from 0.0078125 to 0.03125
- wk_codes: bfloat16 [4096, 128], P('dp', 'tensor'), may hold values from -4 to 4
- wk_scales: float32 [32, 1], replicated, may hold values from 0.0078125 to 0.03125
- wv_codes: bfloat16 [4096, 128], P('dp', 'tensor'), may hold values from -4 to 4
- wv_scales: float32 [32, 1], replicated, may hold values from 0.0078125 to 0.03125
- wo_codes: bfloat16 [1024, 4096], P('tensor', 'dp'), may hold values from -4 to 4
- wo_scales: float32 [8, 32], replicated, may hold values from 0.015625 to 0.0625
Outputs:
- mixed: bfloat16 [6144, 4096], P(('dp', 'tensor'))
All inputs are finite; a program needn't handle non-finite values.
Results may differ from a plain program's by a relative error of at most 0.014.
The roundings to bfloat16 on the way count: a program that leaves them out, or rounds other values in their place, can miss the bound.
Values may be sent and summed in bfloat16 or wider, within the bound.
A program may use at most 64 MiB of HBM per device.

v0:
```python
import jax
import jax.numpy as jnp
from jax import lax
from jax.sharding import PartitionSpec as P

HEAD = 128
BLOCK = 128
SPAN = 384


rope_base = 500000.0
masked_value = -1e30


def from_partner(value, axis, apart):
    mask = 2**apart
    pairs = [(source, source ^ mask) for source in range(lax.axis_size(axis))]
    return lax.ppermute(value, axis, pairs)


def dequantize(codes, scales, row_start, col_start):
    height, breadth = codes.shape
    row_block = (row_start + jnp.arange(height, dtype=jnp.int32)) // BLOCK
    col_block = (col_start + jnp.arange(breadth, dtype=jnp.int32)) // BLOCK
    row_pick = (row_block[:, None] == jnp.arange(scales.shape[0], dtype=jnp.int32)[None, :]).astype(
        jnp.float32
    )
    col_pick = (col_block[None, :] == jnp.arange(scales.shape[1], dtype=jnp.int32)[:, None]).astype(
        jnp.float32
    )
    picked = jnp.dot(row_pick, scales, precision=lax.Precision.HIGHEST)
    expanded = jnp.dot(picked, col_pick, precision=lax.Precision.HIGHEST)
    return (codes.astype(jnp.float32) * expanded).astype(jnp.bfloat16)


def rotate(features, positions):
    half_size = HEAD // 2
    steps = jnp.arange(half_size).astype(jnp.float32)
    inverse = jnp.exp(-(2.0 * steps / HEAD) * jnp.log(jnp.float32(rope_base)))
    angle = positions[:, None] * inverse[None, :]
    cosine = jnp.cos(angle)[:, None, :]
    sine = jnp.sin(angle)[:, None, :]
    first = features[..., :half_size]
    second = features[..., half_size:]
    return jnp.concatenate(
        [first * cosine - second * sine, second * cosine + first * sine], axis=-1
    )


def in_order(upper, mine, partner):
    return jnp.where(
        upper, jnp.concatenate([partner, mine], axis=1), jnp.concatenate([mine, partner], axis=1)
    )


def body(
    tokens, wq_codes, wq_scales, wk_codes, wk_scales, wv_codes, wv_scales, wo_codes, wo_scales
):
    data_index = lax.axis_index("dp")
    head_index = lax.axis_index("tensor")
    weight_rows = wq_codes.shape[0]
    row_start = data_index * weight_rows
    query_width = wq_codes.shape[1]
    shard_width = wk_codes.shape[1]
    wq_local = dequantize(wq_codes, wq_scales, row_start, head_index * query_width)
    wk_local = dequantize(wk_codes, wk_scales, row_start, head_index * shard_width)
    wv_local = dequantize(wv_codes, wv_scales, row_start, head_index * shard_width)
    wo_local = dequantize(
        wo_codes, wo_scales, head_index * wo_codes.shape[0], data_index * wo_codes.shape[1]
    )
    wo_whole = lax.all_gather(wo_local, "dp", axis=1, tiled=True)
    sequence = lax.all_gather(tokens, "tensor", axis=0, tiled=True)
    upper = head_index % 2 == 1
    partner_k, partner_v = from_partner((wk_local, wv_local), "tensor", 0)
    wk_used = in_order(upper, wk_local, partner_k)
    wv_used = in_order(upper, wv_local, partner_v)
    length = sequence.shape[0]
    full_q, full_k, full_v = (
        lax.all_gather(wq_local, "dp", axis=0, tiled=True),
        lax.all_gather(wk_used, "dp", axis=0, tiled=True),
        lax.all_gather(wv_used, "dp", axis=0, tiled=True),
    )
    query_lin = jnp.dot(sequence, full_q, preferred_element_type=jnp.float32)
    key_lin = jnp.dot(sequence, full_k, preferred_element_type=jnp.float32)
    value_lin = jnp.dot(sequence, full_v, preferred_element_type=jnp.float32)
    positions = (jnp.arange(length) % SPAN).astype(jnp.float32)
    heads_here = query_width // HEAD
    span_count = length // SPAN
    queries = rotate(query_lin.reshape(length, heads_here, HEAD), positions).astype(jnp.bfloat16)
    keys = rotate(key_lin.reshape(length, 1, HEAD), positions)[:, 0, :].astype(jnp.bfloat16)
    values = value_lin.astype(jnp.bfloat16)
    queries = queries.reshape(span_count, SPAN, heads_here, HEAD)
    keys = keys.reshape(span_count, SPAN, HEAD)
    values = values.reshape(span_count, SPAN, HEAD)
    causal = jnp.arange(SPAN)[:, None] >= jnp.arange(SPAN)[None, :]
    scores = jnp.einsum("cqhd,ckd->chqk", queries, keys, preferred_element_type=jnp.float32) * (
        1.0 / HEAD**0.5
    )
    scores = jnp.where(causal[None, None, :, :], scores, masked_value)
    peak = jnp.max(scores, axis=-1, keepdims=True)
    powers = jnp.exp(scores - peak)
    total = jnp.sum(powers, axis=-1, keepdims=True)
    probs = (powers / total).astype(jnp.bfloat16)
    attended = (
        jnp.einsum("chqk,ckd->cqhd", probs, values, preferred_element_type=jnp.float32)
        .astype(jnp.bfloat16)
        .reshape(length, query_width)
    )
    terms = jnp.dot(attended, wo_whole, preferred_element_type=jnp.float32)
    mixed = lax.psum_scatter(terms.astype(jnp.bfloat16), "tensor", scatter_dimension=0, tiled=True)
    return mixed


def solution(mesh):
    return jax.shard_map(
        body,
        mesh=mesh,
        in_specs=(
            P(("dp", "tensor"), None),
            P("dp", "tensor"),
            P(),
            P("dp", "tensor"),
            P(),
            P("dp", "tensor"),
            P(),
            P("tensor", "dp"),
            P(),
        ),
        out_specs=P(("dp", "tensor"), None),
        check_vma=False,
    )
```

profile of v0, /device:TPU:0, one launch (start us, length us, event | category | flops | bytes accessed | tf_op | source)
XLA Modules:
  0.0 298.7 jit_solution(14492165854905876810)
XLA Ops:
  6.5 0.0 copy-start
  6.5 0.0 copy-start.3
  6.5 0.0 copy-start.4
  6.5 0.0 all-gather.10.cloned.1.call-start
  6.6 0.9 fusion.18
  7.5 0.9 fusion.17
  8.4 0.9 multiply_convert_fusion.1
  9.3 3.0 %collective-permute-start.1 = (bf16[256,64]{0,1:T(8,128)(2,1)S(1)}, bf16[256,64]{0,1:T(8,128)(2,1)S(1)}, u32[]{:S(2)}, u32[]{:S(2)}) collective-permute-start(bf16[256,64]{0,1:T(8,128)(2,1)S(1)} %get-tuple-element.14), channel_id=1, source_target_pairs={{0,1},{1,0},{2,3},{3,2},{4,5},{5,4},{6,7},{7,6},{8,9},{9,8},{10,11... | collective-permute-start | bytes 98312 | tf_op jit(solution)/shard_map/ppermute | solution.py:18
  12.3 1.9 collective-permute-done.1
  14.2 0.6 maximum_select_fusion.1
  14.9 0.0 all-gather.10.cloned.1.call-update
  14.9 0.0 all-gather.8.cloned.1.call-start
  14.9 0.7 all-gather.8.cloned.1.call-update
  15.6 0.0 all-gather.12.cloned.1.call-start
  15.7 0.9 fusion.16
  16.7 0.0 copy-done.3
  16.7 1.1 fusion.2
  17.7 0.0 all-gather.12.cloned.1.call-update
  17.8 0.0 all-gather.6.cloned.1.call-start
  17.8 2.1 collective-permute-start
  19.9 1.9 collective-permute-done
  21.8 0.6 maximum_select_fusion
  22.4 0.0 all-gather.6.cloned.1.call-update
  22.4 0.0 all-gather.14.cloned.1.call-start
  22.5 0.0 copy-done
  22.5 0.3 fusion.10
  22.8 0.0 copy-done.4
  22.8 1.1 fusion.3
  23.9 0.0 all-gather.14.cloned.1.call-update
  23.9 0.0 reduce-scatter.2.cloned.1.call-start
  24.1 1.4 multiply_cosine_fusion
  25.5 28.1 %all-gather.10.cloned.1.call-done = bf16[4096,128]{0,1:T(8,128)(2,1)} async-done(((bf16[256,128]{0,1:T(8,128)(2,1)}), bf16[4096,128]{0,1:T(8,128)(2,1)}) %all-gather.10.cloned.1.call-update) | async-done | bytes 1048592 | tf_op jit(solution)/shard_map/all_gather | solution.py:80
  53.6 46.0 %all-gather.8.cloned.1.call-done = bf16[384,4096]{1,0:T(8,128)(2,1)} async-done(((bf16[192,4096]{1,0:T(8,128)(2,1)}), bf16[384,4096]{1,0:T(8,128)(2,1)}) %all-gather.8.cloned.1.call-update) | async-done | bytes 3145744 | tf_op jit(solution)/shard_map/all_gather | solution.py:72
  99.6 0.0 copy-start.1
  99.6 3.4 %convolution_bitcast_fusion = f32[384,1,128]{0,2,1:T(8,128)S(1)} fusion(bf16[4096,128]{0,1:T(8,128)(2,1)} %all-gather.10.cloned.1.call-done, bf16[384,4096]{1,0:T(8,128)(2,1)} %all-gather.8.cloned.1.call-done), kind=kOutput, calls=%fused_computation.12 | convolution fusion | flops 402653184 | bytes 4390912 | tf_op jit(solution)/shard_map/dot_general | solution.py:84
  103.1 1.1 fusion.20
  104.1 48.3 %all-gather.12.cloned.1.call-done = bf16[4096,512]{1,0:T(8,128)(2,1)} async-done(((bf16[256,512]{1,0:T(8,128)(2,1)}), bf16[4096,512]{1,0:T(8,128)(2,1)}) %all-gather.12.cloned.1.call-update) | async-done | bytes 4194320 | tf_op jit(solution)/shard_map/all_gather | solution.py:79
  152.4 0.0 copy-done.1
  152.4 4.6 %fusion.37 = f32[512,384]{1,0:T(8,128)S(1)} fusion(bf16[4096,512]{1,0:T(8,128)(2,1)} %all-gather.12.cloned.1.call-done, bf16[384,4096]{1,0:T(8,128)(2,1)S(1)} %copy-done.1), kind=kOutput, calls=%fused_computation.79 | convolution fusion | flops 1610612736 | bytes 8126464 | tf_op jit(solution)/shard_map/dot_general | solution.py:83
  157.0 0.0 copy-start.2
  157.0 0.1 fusion.36
  157.1 0.0 copy-start.5
  157.1 0.3 copy.17
  157.4 0.3 copy.18
  157.6 0.3 copy-done.2
  157.9 0.2 subtract_convert_fusion
  158.1 0.0 copy-done.5
  158.2 0.7 fusion.1
  158.9 0.5 fusion
  159.4 30.4 %all-gather.6.cloned.1.call-done = bf16[4096,128]{0,1:T(8,128)(2,1)} async-done(((bf16[256,128]{0,1:T(8,128)(2,1)}), bf16[4096,128]{0,1:T(8,128)(2,1)}) %all-gather.6.cloned.1.call-update) | async-done | bytes 1048592 | tf_op jit(solution)/shard_map/all_gather | solution.py:81
  189.7 4.1 %convolution_convert_fusion.1 = bf16[128,4,384]{2,0,1:T(8,128)(2,1)S(1)} fusion(f32[384,384,4]{1,0,2:T(8,128)S(1)} %get-tuple-element.16, f32[4,384]{1,0:T(4,128)S(1)} %fusion, f32[4,384]{1,0:T(4,128)S(1)} %get-tuple-element.15, pred[384,384]{0,1:T(8,128)(4,1)S(1)} %iota_compare_fusion, bf16[4096,128]{0,1:T(8,128)(2,1)} %all-gather.6.cloned.1.call-done, ...), kind=kOutput, calls=%fused_computation.6 | convolution fusion | flops 556843008 | bytes 7106560 | tf_op jit(solution)/shard_map/chqk,ckd->cqhd/dot_general | solution.py:105
  193.8 50.7 %all-gather.14.cloned.1.call-done = bf16[512,4096]{1,0:T(8,128)(2,1)} async-done(((bf16[512,256]{1,0:T(8,128)(2,1)}), bf16[512,4096]{1,0:T(8,128)(2,1)}) %all-gather.14.cloned.1.call-update) | async-done | bytes 4194320 | tf_op jit(solution)/shard_map/all_gather | solution.py:71
  244.5 5.7 %convolution_convert_fusion = bf16[384,4096]{1,0:T(8,128)(2,1)} fusion(bf16[384,512]{0,1:T(8,128)(2,1)S(1)} %bitcast.58, bf16[512,4096]{1,0:T(8,128)(2,1)} %all-gather.14.cloned.1.call-done), kind=kOutput, calls=%fused_computation | convolution fusion | flops 1612185600 | bytes 7733248 | tf_op jit(solution)/shard_map/dot_general | solution.py:109
  250.2 0.0 reduce-scatter.2.cloned.1.call-update
  250.2 41.7 %reduce-scatter.2.cloned.1.call-done = bf16[192,4096]{1,0:T(8,128)(2,1)} async-done(((bf16[384,4096]{1,0:T(8,128)(2,1)}), bf16[192,4096]{1,0:T(8,128)(2,1)}) %reduce-scatter.2.cloned.1.call-update) | async-done | bytes 1572880 | tf_op jit(solution)/shard_map/reduce_scatter | solution.py:110
  (6 shorter events, 0.1 us)
Async XLA Ops:
  6.5 16.0 %copy-start = (f32[8,32]{1,0:T(8,128)S(1)}, f32[8,32]{1,0:T(8,128)}, u32[]{:S(2)}) copy-start(f32[8,32]{1,0:T(8,128)} %param.17) | copy-start | bytes 3076
  6.5 10.1 %copy-start.3 = (bf16[256,512]{1,0:T(8,128)(2,1)S(1)}, bf16[256,512]{1,0:T(8,128)(2,1)}, u32[]{:S(2)}) copy-start(bf16[256,512]{1,0:T(8,128)(2,1)} %param.10) | copy-start | bytes 786436
  6.5 16.3 %copy-start.4 = (bf16[512,256]{1,0:T(8,128)(2,1)S(1)}, bf16[512,256]{1,0:T(8,128)(2,1)}, u32[]{:S(2)}) copy-start(bf16[512,256]{1,0:T(8,128)(2,1)} %param.16) | copy-start | bytes 786436
  6.5 47.1 %all-gather.10.cloned.1.call-start = ((), (), s32[]{:S(2)}) async-start(), calls=%async_computation.3 | async-start | bytes 1114112 | tf_op jit(solution)/shard_map/all_gather | solution.py:80
  9.3 4.9 %collective-permute-start.1 = (bf16[256,64]{0,1:T(8,128)(2,1)S(1)}, bf16[256,64]{0,1:T(8,128)(2,1)S(1)}, u32[]{:S(2)}, u32[]{:S(2)}) collective-permute-start(bf16[256,64]{0,1:T(8,128)(2,1)S(1)} %get-tuple-element.14), channel_id=1, source_target_pairs={{0,1},{1,0},{2,3},{3,2},{4,5},{5,4},{6,7},{7,6},{8,9},{9,8},{10,11... | collective-permute-start | bytes 98312 | tf_op jit(solution)/shard_map/ppermute | solution.py:18
  14.9 84.7 %all-gather.8.cloned.1.call-start = ((), (), s32[]{:S(2)}) async-start(), calls=%async_computation.2 | async-start | bytes 4718592 | tf_op jit(solution)/shard_map/all_gather | solution.py:72
  15.6 136.8 %all-gather.12.cloned.1.call-start = ((), (), s32[]{:S(2)}) async-start(), calls=%async_computation.4 | async-start | bytes 4456448 | tf_op jit(solution)/shard_map/all_gather | solution.py:79
  17.8 172.0 %all-gather.6.cloned.1.call-start = ((), (), s32[]{:S(2)}) async-start(), calls=%async_computation.1 | async-start | bytes 1114112 | tf_op jit(solution)/shard_map/all_gather | solution.py:81
  17.8 4.0 %collective-permute-start = (bf16[256,64]{0,1:T(8,128)(2,1)S(1)}, bf16[256,64]{0,1:T(8,128)(2,1)S(1)}, u32[]{:S(2)}, u32[]{:S(2)}) collective-permute-start(bf16[256,64]{0,1:T(8,128)(2,1)S(1)} %get-tuple-element.13), channel_id=1, source_target_pairs={{0,1},{1,0},{2,3},{3,2},{4,5},{5,4},{6,7},{7,6},{8,9},{9,8},{10,11... | collective-permute-start | bytes 98312 | tf_op jit(solution)/shard_map/ppermute | solution.py:18
  22.4 222.0 %all-gather.14.cloned.1.call-start = ((), (), s32[]{:S(2)}) async-start(), calls=%async_computation.5 | async-start | bytes 4456448 | tf_op jit(solution)/shard_map/all_gather | solution.py:71
  23.9 267.9 %reduce-scatter.2.cloned.1.call-start = ((), (), s32[]{:S(2)}) async-start(), calls=%async_computation.6 | async-start | bytes 4718592 | tf_op jit(solution)/shard_map/reduce_scatter | solution.py:110
  99.6 52.8 %copy-start.1 = (bf16[384,4096]{1,0:T(8,128)(2,1)S(1)}, bf16[384,4096]{1,0:T(8,128)(2,1)}, u32[]{:S(2)}) copy-start(bf16[384,4096]{1,0:T(8,128)(2,1)} %all-gather.8.cloned.1.call-done) | copy-start | bytes 9437188
  157.0 0.9 copy-start.2
  157.1 1.1 copy-start.5
Sparse Core Ops, SparseCore 0:
  15.0 38.5 all-gather.9
  55.2 44.4 all-gather.7
  101.8 50.5 all-gather.11
  154.4 35.2 all-gather.5
  191.7 52.6 all-gather.13
  250.3 41.4 reduce-scatter.1
where the time goes:
time: 299 us
  waiting for transfers between devices  250 us (84%)
  matrix products  23.7 us (8%)
  between operations  13.7 us (5%)
  other arithmetic  5.51 us (2%)
  starting transfers between devices  5.3 us (2%)
    all_gather x1, waiting for transfers between devices, body(): wo_whole = lax.all_gather(wo_local, 'dp', axis=1, tiled=True)  50.7 us
    all_gather x1, waiting for transfers between devices, body(): lax.all_gather(wq_local, 'dp', axis=0, tiled=True)  48.3 us
    all_gather x1, waiting for transfers between devices, body(): sequence = lax.all_gather(tokens, 'tensor', axis=0, tiled=True)  46 us
    reduce_scatter x1, waiting for transfers between devices, body(): lax.psum_scatter(terms.astype(jnp.bfloat16), 'tensor', scatter_dimension=...  41.7 us
    all_gather x1, waiting for transfers between devices, body(): lax.all_gather(wv_used, 'dp', axis=0, tiled=True)  30.4 us
    all_gather x1, waiting for transfers between devices, body(): lax.all_gather(wk_used, 'dp', axis=0, tiled=True)  28.1 us
  transfers between devices with their start and end apart: 8, of which 8 were waited for; matrix products, arithmetic and copies ran while one was open for 7% of the time, Pallas kernels for 0%

commit v1 on v0

--- a/solution.py
+++ b/solution.py
@@ -1,6 +1,9 @@
 import jax
 import jax.numpy as jnp
+import numpy as np
 from jax import lax
+from jax.experimental import pallas as pl
+from jax.experimental.pallas import tpu as pltpu
 from jax.sharding import PartitionSpec as P
 
 HEAD = 128
@@ -111,9 +114,307 @@
     return mixed
 
 
+MESH = pl.DeviceIdType.MESH
+Z, Y, CORES = 4, 2, 2
+ROWS = 192
+DEPTH = 256
+WIDTH = 512
+MODEL = 4096
+TOKEN_PIECES = 4
+
+
+def rope_tables():
+    steps = np.arange(HEAD // 2, dtype=np.float64)
+    inverse = rope_base ** (-2.0 * steps / HEAD)
+    angle = np.arange(SPAN, dtype=np.float64)[:, None] * inverse[None, :]
+    cosine, sine = np.cos(angle), np.sin(angle)
+    return (
+        np.concatenate([cosine, cosine], axis=1).astype(np.float32),
+        np.concatenate([-sine, sine], axis=1).astype(np.float32),
+    )
+
+
+def scaled(codes, scale):
+    return (codes.astype(jnp.float32) * scale).astype(jnp.bfloat16)
+
+
+def fused_kernel(
+    tokens, wq, wq_s, wk, wk_s, wv, wv_s, wo, wo_s, cos_ref, sin_ref, out,
+    seq, wqkv, wob, kv_pair, acc, q_buf, k_buf, v_buf, att, sent, got, kept,
+    z_send, z_recv, y_send, y_recv, c_send, c_recv, t_send, t_recv, t_local, kv_send, kv_recv, o_send, o_recv,
+):
+    me = lax.axis_index("dp")
+    x = lax.axis_index("tensor")
+    core = me % CORES
+    y = (me // CORES) % Y
+    z = me // (CORES * Y)
+    across = 1 - x
+
+    def index(zz, yy, cc):
+        return (zz * Y + yy) * CORES + cc
+
+    def block(i, cc):
+        return index((z - i + 8) % Z, (y + i // 4) % Y, cc)
+
+    y_dev = (index(z, 1 - y, core), x)
+    c_dev = (index(z, y, 1 - core), x)
+    x_dev = (me, across)
+    z_devs = [(index((z + k) % Z, y, core), x) for k in range(1, Z)]
+
+    barrier = pltpu.get_barrier_semaphore()
+    for dev in [x_dev, y_dev, c_dev] + z_devs:
+        pl.semaphore_signal(barrier, inc=1, device_id=dev, device_id_type=MESH)
+
+    mine_rows = pl.multiple_of(x * ROWS, 16)
+    other_rows = pl.multiple_of(across * ROWS, 16)
+    local = pltpu.make_async_copy(tokens, seq.at[pl.ds(mine_rows, ROWS), :], t_local)
+    local.start()
+
+    def slot(piece, d):
+        if piece < 3:
+            return wqkv.at[piece, pl.ds(pl.multiple_of(d * DEPTH, DEPTH), DEPTH), :]
+        return wob.at[piece - 3, :, pl.ds(pl.multiple_of(d * 128, 128), 128)]
+
+    def remote(ref, send, recv, dev):
+        return pltpu.make_async_remote_copy(
+            src_ref=ref, dst_ref=ref, send_sem=send, recv_sem=recv, device_id=dev, device_id_type=MESH
+        )
+
+    def along_z(piece, k, d):
+        return remote(slot(piece, d), z_send.at[piece, k - 1], z_recv.at[piece, k - 1], z_devs[k - 1])
+
+    def along_y(piece, i, d):
+        return remote(slot(piece, d), y_send.at[piece, i], y_recv.at[piece, i], y_dev)
+
+    def to_core(piece, i, d):
+        return remote(slot(piece, d), c_send.at[piece, i], c_recv.at[piece, i], c_dev)
+
+    sends = []
+
+    def go(copy):
+        copy.start()
+        sends.append(copy)
+
+    def send_own(piece):
+        for k in (2, 1, 3):
+            go(along_z(piece, k, me))
+        go(along_y(piece, 0, me))
+        go(to_core(piece, 0, me))
+
+    def forward_z(piece):
+        for k in (1, 3, 2):
+            d = block(k, core)
+            along_z(piece, k, d).wait_recv()
+            go(along_y(piece, k, d))
+            go(to_core(piece, k, d))
+
+    def forward_y(piece):
+        for i in range(4):
+            d = block(4 + i, core)
+            along_y(piece, i, d).wait_recv()
+            go(to_core(piece, 4 + i, d))
+
+    row0 = me * DEPTH
+    for i in range(2):
+        rows = pl.ds(i * 128, 128)
+        kv_pair[0, rows, :] = jnp.concatenate(
+            [scaled(wk[rows, :], wk_s[2 * me + i, 0]), scaled(wv[rows, :], wv_s[2 * me + i, 0])], axis=1
+        )
+        place = pl.ds(pl.multiple_of(row0 + i * 128, 128), 128)
+        for j in range(4):
+            wqkv[2 * (j // 2), place, pl.ds((j % 2) * 128, 128)] = scaled(
+                wq[rows, pl.ds(j * 128, 128)], wq_s[2 * me + i, 4 * x + j]
+            )
+
+    pl.semaphore_wait(barrier, 6)
+    kv_copy = pltpu.make_async_remote_copy(
+        src_ref=kv_pair.at[0], dst_ref=kv_pair.at[1], send_sem=kv_send, recv_sem=kv_recv,
+        device_id=x_dev, device_id_type=MESH,
+    )
+    go(kv_copy)
+    part = ROWS // TOKEN_PIECES
+    token_copies = []
+    for t in range(TOKEN_PIECES):
+        copy = pltpu.make_async_remote_copy(
+            src_ref=tokens.at[pl.ds(t * part, part), :],
+            dst_ref=seq.at[pl.ds(pl.multiple_of(mine_rows + t * part, 16), part), :],
+            send_sem=t_send.at[t], recv_sem=t_recv.at[t], device_id=x_dev, device_id_type=MESH,
+        )
+        go(copy)
+        token_copies.append(copy)
+    send_own(0)
+
+    kv_copy.wait_recv()
+    own_rows = pl.ds(pl.multiple_of(row0, DEPTH), DEPTH)
+    own_kv, far_kv = kv_pair[0], kv_pair[1]
+    low = jnp.where(x == 0, own_kv, far_kv)
+    high = jnp.where(x == 0, far_kv, own_kv)
+    wqkv[1, own_rows, :] = jnp.concatenate([low[:, :64], high[:, :64], low[:, 64:], high[:, 64:]], axis=1)
+    send_own(1)
+    send_own(2)
+
+    for h in range(2):
+        for i in range(4):
+            rows = pl.ds(i * 128, 128)
+            wob[h, rows, pl.ds(pl.multiple_of(me * 128, 128), 128)] = scaled(
+                wo[rows, pl.ds(h * 128, 128)], wo_s[4 * x + i, 2 * me + h]
+            )
+
+    forward_z(0)
+    forward_z(1)
+    forward_y(0)
+    forward_z(2)
+    send_own(3)
+    forward_y(1)
+    send_own(4)
+    forward_y(2)
+
+    def project(piece):
+        for i in range(8):
+            to_core(piece, i, block(i, 1 - core)).wait_recv()
+        acc[...] = jnp.zeros_like(acc)
+
+        def step(s, carry):
+            cut = pl.ds(pl.multiple_of(s * 1024, 1024), 1024)
+            acc[...] += jnp.dot(seq[:, cut], wqkv[piece, cut, :], preferred_element_type=jnp.float32)
+            return carry
+
+        lax.fori_loop(0, MODEL // 1024, step, 0)
+
+    def roped(cols):
+        u = acc[:, cols]
+        return (u * cos_ref[...] + pltpu.roll(u, 64, 1) * sin_ref[...]).astype(jnp.bfloat16)
+
+    def attend(h):
+        for b in range(3):
+            rows = pl.ds(b * 128, 128)
+            width = (b + 1) * 128
+            scores = lax.dot_general(
+                q_buf[h, rows, :], k_buf[pl.ds(0, width), :], (((1,), (1,)), ((), ())),
+                preferred_element_type=jnp.float32,
+            ) * (1.0 / HEAD**0.5)
+            at_row = b * 128 + lax.broadcasted_iota(jnp.int32, (128, width), 0)
+            at_col = lax.broadcasted_iota(jnp.int32, (128, width), 1)
+            scores = jnp.where(at_row >= at_col, scores, masked_value)
+            powers = jnp.exp(scores - jnp.max(scores, axis=-1, keepdims=True))
+            total = jnp.sum(powers, axis=-1, keepdims=True)
+            probs = (powers / total).astype(jnp.bfloat16)
+            att[rows, pl.ds(h * 128, 128)] = jnp.dot(
+                probs, v_buf[pl.ds(0, width), :], preferred_element_type=jnp.float32
+            ).astype(jnp.bfloat16)
+
+    local.wait()
+    for copy in token_copies:
+        copy.wait_recv()
+    project(0)
+    for h in range(2):
+        q_buf[h] = roped(slice(h * 128, h * 128 + 128))
+    project(1)
+    k_buf[...] = roped(slice(0, 128))
+    v_buf[...] = acc[:, 128:].astype(jnp.bfloat16)
+    attend(0)
+    attend(1)
+    project(2)
+    for h in range(2):
+        q_buf[2 + h] = roped(slice(h * 128, h * 128 + 128))
+    forward_z(3)
+    attend(2)
+    attend(3)
+    forward_z(4)
+
+    def out_copy(j):
+        return pltpu.make_async_remote_copy(
+            src_ref=sent.at[j], dst_ref=got.at[j], send_sem=o_send.at[j], recv_sem=o_recv.at[j],
+            device_id=x_dev, device_id_type=MESH,
+        )
+
+    def chip(i):
+        return block(i, 0) // 2
+
+    def produce(h, start):
+        def step(i, carry):
+            to_core(3 + h, i, block(i, 1 - core)).wait_recv()
+            j = h * 8 + i
+            w = wob[h, :, pl.ds(pl.multiple_of(chip(i) * 256, 256), 256)]
+            sent[j] = jnp.dot(
+                att[pl.ds(other_rows, ROWS), :], w, preferred_element_type=jnp.float32
+            ).astype(jnp.bfloat16)
+            out_copy(j).start()
+            kept[j] = jnp.dot(
+                att[pl.ds(mine_rows, ROWS), :], w, preferred_element_type=jnp.float32
+            ).astype(jnp.bfloat16)
+            return carry
+
+        lax.fori_loop(start, start + 4, step, 0)
+
+    produce(0, 0)
+    forward_y(3)
+    produce(0, 4)
+    produce(1, 0)
+    forward_y(4)
+    produce(1, 4)
+
+    def finish(j, carry):
+        h = j // 8
+        i = j % 8
+        out_copy(j).wait_recv()
+        total = (kept[j].astype(jnp.float32) + got[j].astype(jnp.float32)).astype(jnp.bfloat16)
+        base = chip(i) * 512 + h * 128
+        out[:, pl.ds(pl.multiple_of(base, 128), 128)] = total[:, :128]
+        out[:, pl.ds(pl.multiple_of(base + 256, 128), 128)] = total[:, 128:]
+        return carry
+
+    lax.fori_loop(0, 16, finish, 0)
+    for copy in sends:
+        copy.wait_send()
+
+    def drain(j, carry):
+        out_copy(j).wait_send()
+        return carry
+
+    lax.fori_loop(0, 16, drain, 0)
+
+
+def fused_body(tokens, wq, wq_s, wk, wk_s, wv, wv_s, wo, wo_s):
+    cosine, sine = rope_tables()
+    vmem = pl.BlockSpec(memory_space=pltpu.VMEM)
+    smem = pl.BlockSpec(memory_space=pltpu.SMEM)
+    hbm = pl.BlockSpec(memory_space=pl.ANY)
+    dma = pltpu.SemaphoreType.DMA
+    bf16 = jnp.bfloat16
+    return pl.pallas_call(
+        fused_kernel,
+        out_shape=jax.ShapeDtypeStruct((ROWS, MODEL), bf16),
+        in_specs=[hbm, vmem, smem, vmem, smem, vmem, smem, vmem, smem, vmem, vmem],
+        out_specs=vmem,
+        scratch_shapes=[
+            pltpu.VMEM((SPAN, MODEL), bf16),
+            pltpu.VMEM((3, MODEL, 256), bf16),
+            pltpu.VMEM((2, WIDTH, MODEL // 2), bf16),
+            pltpu.VMEM((2, DEPTH, 128), bf16),
+            pltpu.VMEM((SPAN, 256), jnp.float32),
+            pltpu.VMEM((4, SPAN, HEAD), bf16),
+            pltpu.VMEM((SPAN, HEAD), bf16),
+            pltpu.VMEM((SPAN, HEAD), bf16),
+            pltpu.VMEM((SPAN, WIDTH), bf16),
+            pltpu.VMEM((16, ROWS, 256), bf16),
+            pltpu.VMEM((16, ROWS, 256), bf16),
+            pltpu.VMEM((16, ROWS, 256), bf16),
+            dma((5, 3)), dma((5, 3)), dma((5, 4)), dma((5, 4)), dma((5, 8)), dma((5, 8)),
+            dma((TOKEN_PIECES,)), dma((TOKEN_PIECES,)), dma, dma, dma, dma((16,)), dma((16,)),
+        ],
+        compiler_params=pltpu.CompilerParams(
+            collective_id=0, has_side_effects=True, vmem_limit_bytes=48 * 1024 * 1024
+        ),
+        cost_estimate=pl.CostEstimate(flops=4_500_000_000, bytes_accessed=6_000_000, transcendentals=300_000),
+    )(tokens, wq, wq_s, wk, wk_s, wv, wv_s, wo, wo_s, jnp.asarray(cosine), jnp.asarray(sine))
+
+
 def solution(mesh):
+
+    fits = mesh.shape["dp"] == Z * Y * CORES and mesh.shape["tensor"] == 2
     return jax.shard_map(
-        body,
+        fused_body if fits else body,
         mesh=mesh,
         in_specs=(
             P(("dp", "tensor"), None),

time: 299 us -> 111 us (0.37)
  the two profiles are of different devices: /device:TPU:0 before, /device:TPU:16 now
where the time goes in v1:
time: 111 us
  Pallas kernels  99.8 us (90%)
  local copies, waits for them, and re-layouts  11 us (10%)
    pallas_call x1, Pallas kernels, fused_body(): pl.pallas_call(fused_kernel, out_shape=jax.ShapeDtypeStruct((ROWS, MODEL)...  99.8 us
    unnamed x18, local copies, waits for them, and re-layouts  11 us

profile of v1, /device:TPU:16, one launch (start us, length us, event | category | flops | bytes accessed | tf_op | source)
XLA Modules:
  0.0 110.8 jit_solution(15588090764263899101)
XLA Ops:
  0.0 0.8 copy.12.wq_s
  0.8 0.7 copy.14.wk_s
  1.5 0.7 copy.16.wv_s
  2.2 0.9 copy.13.wk
  3.1 0.9 copy.15.wv
  4.0 0.0 copy-start
  4.0 1.4 %copy-done = bf16[192,4096]{1,0:T(8,128)(2,1)S(1)} copy-done((bf16[192,4096]{1,0:T(8,128)(2,1)S(1)}, bf16[192,4096]{1,0:T(8,128)(2,1)}, u32[]{:S(2)}) %copy-start) | copy-done | bytes 1572888
  5.4 0.0 copy-start.1
  5.4 0.9 copy-done.1
  6.4 0.0 copy-start.2
  6.4 0.9 copy-done.2
  7.3 0.0 copy-start.3
  7.3 0.7 copy-done.3
  8.0 0.0 copy-start.4
  8.0 0.9 copy-done.4
  8.9 0.0 copy-start.5
  8.9 0.9 copy-done.5
  9.8 99.8 %shard_map.109 = bf16[192,4096]{1,0:T(8,128)(2,1)S(1)} custom-call(bf16[192,4096]{1,0:T(8,128)(2,1)S(1)} %copy-done, bf16[256,512]{1,0:T(8,128)(2,1)S(1)} %copy-done.1, f32[32,8]{1,0:T(8,128)S(1)} %copy.12.wq_s, bf16[256,64]{1,0:T(8,128)(2,1)S(1)} %copy.13.wk, f32[32,1]{1,0:T(8,128)S(1)} %copy.14.wk_s, bf16[256,64]{1,0:T(8,128)(2,1)S(1)} %copy.15.wv, ...), custom_call_target="tpu_custom_call" | custom-call | flops 4499999744 | bytes 6000000 | tf_op jit(solution)/shard_map/pallas_call | solution.py:385
  109.7 1.1 %copy.18 = bf16[192,4096]{1,0:T(8,128)(2,1)} copy(bf16[192,4096]{1,0:T(8,128)(2,1)S(1)} %shard_map.109) | data formatting | bytes 3145728
Async XLA Ops:
  4.0 1.4 %copy-start = (bf16[192,4096]{1,0:T(8,128)(2,1)S(1)}, bf16[192,4096]{1,0:T(8,128)(2,1)}, u32[]{:S(2)}) copy-start(bf16[192,4096]{1,0:T(8,128)(2,1)} %tokens.1) | copy-start | bytes 4718596
  5.4 0.9 copy-start.1
  6.4 0.9 copy-start.2
  7.3 0.7 copy-start.3
  8.0 0.9 copy-start.4
  8.9 0.9 copy-start.5

commit v2 on v0

--- a/solution.py
+++ b/solution.py
@@ -1,6 +1,9 @@
 import jax
 import jax.numpy as jnp
+import numpy as np
 from jax import lax
+from jax.experimental import pallas as pl
+from jax.experimental.pallas import tpu as pltpu
 from jax.sharding import PartitionSpec as P
 
 HEAD = 128
@@ -111,9 +114,403 @@
     return mixed
 
 
+MESH = pl.DeviceIdType.MESH
+Z, Y, CORES = 4, 2, 2
+ROWS = 192
+DEPTH = 256
+WIDTH = 512
+MODEL = 4096
+TOKEN_PIECES = 4
+VMEM_BYTES = 62 * 1024 * 1024
+
+
+def rope_tables():
+    steps = np.arange(HEAD // 2, dtype=np.float64)
+    inverse = rope_base ** (-2.0 * steps / HEAD)
+    angle = np.arange(SPAN, dtype=np.float64)[:, None] * inverse[None, :]
+    cosine, sine = np.cos(angle), np.sin(angle)
+    return (
+        np.concatenate([cosine, cosine], axis=1).astype(np.float32),
+        np.concatenate([-sine, sine], axis=1).astype(np.float32),
+    )
+
+
+def scaled(codes, scale):
+    return (codes.astype(jnp.float32) * scale).astype(jnp.bfloat16)
+
+
+def fused_kernel(
+    tokens, wq_h, wq_sh, wk_h, wk_sh, wv_h, wv_sh, wo_h, wo_sh, cos_h, sin_h, out,
+    wq, wk, wv, wo, cos_ref, sin_ref, wq_s, wk_s, wv_s, wo_s,
+    seq, wqkv, wkv, wob, kv_half, kv_far, acc, q_buf, k_buf, v_buf, att, sent, got,
+    z_send, z_recv, y_send, y_recv, c_send, c_recv, t_send, t_recv, in_sem, kv_send, kv_recv, o_send, o_recv,
+):
+    me = lax.axis_index("dp")
+    x = lax.axis_index("tensor")
+    core = me % CORES
+    y = (me // CORES) % Y
+    z = me // (CORES * Y)
+    across = 1 - x
+
+    def index(zz, yy, cc):
+        return (zz * Y + yy) * CORES + cc
+
+    def block(i, cc):
+        return index((z - i + 8) % Z, (y + i // 4) % Y, cc)
+
+    y_dev = (index(z, 1 - y, core), x)
+    c_dev = (index(z, y, 1 - core), x)
+    x_dev = (me, across)
+    z_devs = [(index((z + k) % Z, y, core), x) for k in range(1, Z)]
+
+    barrier = pltpu.get_barrier_semaphore()
+    for dev in [x_dev, y_dev, c_dev] + z_devs:
+        pl.semaphore_signal(barrier, inc=1, device_id=dev, device_id_type=MESH)
+
+    mine_rows = pl.multiple_of(x * ROWS, 64)
+    other_rows = pl.multiple_of(across * ROWS, 64)
+    pairs = [
+        (wk_h, wk), (wv_h, wv), (wk_sh, wk_s), (wv_sh, wv_s), (wq_sh, wq_s), (wq_h, wq),
+        (wo_h, wo), (wo_sh, wo_s), (cos_h, cos_ref), (sin_h, sin_ref),
+        (tokens, seq.at[pl.ds(mine_rows, ROWS), :]),
+    ]
+    loads = [pltpu.make_async_copy(a, b, in_sem.at[i]) for i, (a, b) in enumerate(pairs)]
+    for load in loads:
+        load.start()
+
+    def slot(part, d):
+        piece, r = part // 2, part % 2
+        if piece == 1:
+            return wkv.at[pl.ds(pl.multiple_of(d * DEPTH, DEPTH), DEPTH), :]
+        if piece < 3:
+            return wqkv.at[piece // 2, pl.ds(pl.multiple_of(d * DEPTH + r * 128, 128), 128), :]
+        return wob.at[piece - 3, pl.ds(r * 256, 256), pl.ds(pl.multiple_of(d * 128, 128), 128)]
+
+    def remote(ref, send, recv, dev):
+        return pltpu.make_async_remote_copy(
+            src_ref=ref, dst_ref=ref, send_sem=send, recv_sem=recv, device_id=dev, device_id_type=MESH
+        )
+
+    def along_z(part, d, send, recv, step):
+        to = (index((z + step + Z) % Z, y, core), x)
+        return remote(slot(part, d), z_send.at[part, send], z_recv.at[part, recv], to)
+
+    def along_y(part, i, d):
+        return remote(slot(part, d), y_send.at[part, i], y_recv.at[part, i], y_dev)
+
+    def to_core(part, i, d):
+        return remote(slot(part, d), c_send.at[part, i], c_recv.at[part, i], c_dev)
+
+    sends = []
+
+    def go(copy):
+        copy.start()
+        sends.append(copy)
+
+    maybe = []
+
+    def go_if(condition, copy):
+        pl.when(condition)(copy.start)
+        maybe.append((condition, copy))
+
+    arrival = [
+        jnp.where(z == 0, 3, 1),
+        jnp.where((z == 0) | (z == 3), 2, 3),
+        jnp.where(z == 0, 1, jnp.where(z == 3, 3, 2)),
+    ]
+
+    def own_z(part):
+        go_if(z < Z - 1, along_z(part, me, 0, 0, 1))
+        go_if(z > 0, along_z(part, me, 1, 2, -1))
+
+    def own_yc(part):
+        go(along_y(part, 0, me))
+        go(to_core(part, 0, me))
+
+    def forward_z(part):
+        for n, i in enumerate(arrival):
+            d = block(i, core)
+            along_z(part, d, 0, i - 1, 1).wait_recv()
+            go_if((i <= z) & (z < Z - 1), along_z(part, d, 2 + n, jnp.minimum(i, 2), 1))
+            go_if((i > z) & (z > 0), along_z(part, d, 2 + n, jnp.maximum(i - 2, 0), -1))
+            go(along_y(part, i, d))
+            go(to_core(part, i, d))
+
+    def forward_y(part):
+        for i in range(4):
+            d = block(4 + i, core)
+            along_y(part, i, d).wait_recv()
+            go(to_core(part, 4 + i, d))
+
+    pl.semaphore_wait(barrier, 6)
+    part_rows = ROWS // TOKEN_PIECES
+    token_copies = []
+    for t in range(TOKEN_PIECES):
+        copy = pltpu.make_async_remote_copy(
+            src_ref=tokens.at[pl.ds(t * part_rows, part_rows), :],
+            dst_ref=seq.at[pl.ds(pl.multiple_of(mine_rows + t * part_rows, 16), part_rows), :],
+            send_sem=t_send.at[t], recv_sem=t_recv.at[t], device_id=x_dev, device_id_type=MESH,
+        )
+        go(copy)
+        token_copies.append(copy)
+
+    row0 = me * DEPTH
+
+    def scale_q(piece):
+        for i in range(2):
+            place = pl.ds(pl.multiple_of(row0 + i * 128, 128), 128)
+            for j in range(2):
+                wqkv[piece // 2, place, pl.ds(j * 128, 128)] = scaled(
+                    wq[pl.ds(i * 128, 128), pl.ds(piece * 128 + j * 128, 128)],
+                    wq_s[4 * x + piece + j, 2 * me + i],
+                )
+            own_yc(2 * piece + i)
+            if piece == 0:
+                own_z(i)
+
+    loads[4].wait()
+    loads[5].wait()
+    scale_q(0)
+    for i in range(4):
+        loads[i].wait()
+    for i in range(2):
+        rows = pl.ds(i * 128, 128)
+        both = jnp.concatenate(
+            [
+                wk[:, rows].astype(jnp.float32) * wk_s[0, 2 * me + i],
+                wv[:, rows].astype(jnp.float32) * wv_s[0, 2 * me + i],
+            ],
+            axis=0,
+        )
+        wkv[pl.ds(pl.multiple_of(row0 + i * 128, 128), 128), :] = both.T.astype(jnp.bfloat16)
+    own_yc(2)
+    own_z(2)
+    scale_q(2)
+
+    loads[6].wait()
+    loads[7].wait()
+    for h in range(2):
+        for i in range(4):
+            rows = pl.ds(i * 128, 128)
+            wob[h, rows, pl.ds(pl.multiple_of(me * 128, 128), 128)] = scaled(
+                wo[rows, pl.ds(h * 128, 128)], wo_s[4 * x + i, 2 * me + h]
+            )
+    for i in range(8, 11):
+        loads[i].wait()
+
+    def arrived(piece):
+        for part in (2,) if piece == 1 else (2 * piece, 2 * piece + 1):
+            for i in range(8):
+                to_core(part, i, block(i, 1 - core)).wait_recv()
+
+    def project(total, weights, row):
+        rows = pl.ds(row, ROWS)
+        total[rows, :] = jnp.zeros((ROWS, total.shape[1]), jnp.float32)
+
+        def step(s, carry):
+            cut = pl.ds(pl.multiple_of(s * 1024, 1024), 1024)
+            total[rows, :] += jnp.dot(seq[rows, cut], weights[cut, :], preferred_element_type=jnp.float32)
+            return carry
+
+        lax.fori_loop(0, MODEL // 1024, step, 0)
+
+    def roped(u, row):
+        rows = pl.ds(row, ROWS)
+        return (u * cos_ref[rows, :] + pltpu.roll(u, 64, 1) * sin_ref[rows, :]).astype(jnp.bfloat16)
+
+    def take_q(piece, row):
+        rows = pl.ds(row, ROWS)
+        project(acc, wqkv.at[piece // 2], row)
+        q_buf[piece, rows, :] = roped(acc[rows, :128], row)
+        q_buf[piece + 1, rows, :] = roped(acc[rows, 128:], row)
+
+    def kv_copy(n, row):
+        rows = pl.ds(row, ROWS)
+        return pltpu.make_async_remote_copy(
+            src_ref=kv_half.at[rows, :], dst_ref=kv_far.at[rows, :], send_sem=kv_send.at[n], recv_sem=kv_recv.at[n],
+            device_id=x_dev, device_id_type=MESH,
+        )
+
+    def take_kv(n, row):
+        project(kv_half, wkv, row)
+        go(kv_copy(n, row))
+
+    def join_kv(row):
+        rows = pl.ds(row, ROWS)
+        own_kv, far_kv = kv_half[rows, :], kv_far[rows, :]
+        low = jnp.where(x == 0, own_kv, far_kv)
+        high = jnp.where(x == 0, far_kv, own_kv)
+        k_buf[rows, :] = roped(jnp.concatenate([low[:, :64], high[:, :64]], axis=1), row)
+        v_buf[rows, :] = jnp.concatenate([low[:, 64:], high[:, 64:]], axis=1).astype(jnp.bfloat16)
+
+    def attend(h, row):
+        rows = pl.ds(row, ROWS)
+        scores = lax.dot_general(
+            q_buf[h, rows, :], k_buf[...], (((1,), (1,)), ((), ())), preferred_element_type=jnp.float32
+        ) * (1.0 / HEAD**0.5)
+        at_row = row + lax.broadcasted_iota(jnp.int32, (ROWS, SPAN), 0)
+        at_col = lax.broadcasted_iota(jnp.int32, (ROWS, SPAN), 1)
+        scores = jnp.where(at_row >= at_col, scores, masked_value)
+        powers = jnp.exp(scores - jnp.max(scores, axis=-1, keepdims=True))
+        total = jnp.sum(powers, axis=-1, keepdims=True)
+        probs = (powers * (1.0 / total)).astype(jnp.bfloat16)
+        att[rows, pl.ds(h * 128, 128)] = jnp.dot(
+            probs, v_buf[...], preferred_element_type=jnp.float32
+        ).astype(jnp.bfloat16)
+
+    forward_z(0)
+    own_z(4)
+    forward_z(1)
+    own_z(5)
+    forward_y(0)
+    forward_z(2)
+    own_z(6)
+    own_yc(6)
+    forward_y(1)
+    forward_z(4)
+    own_z(7)
+    own_yc(7)
+    forward_y(2)
+    arrived(0)
+    take_q(0, mine_rows)
+    forward_z(5)
+    own_z(8)
+    own_yc(8)
+    forward_y(4)
+    arrived(1)
+    take_kv(0, mine_rows)
+    forward_z(6)
+    own_z(9)
+    own_yc(9)
+    forward_z(7)
+    forward_y(5)
+    forward_z(8)
+    for copy in token_copies:
+        copy.wait_recv()
+    take_kv(1, other_rows)
+    take_q(0, other_rows)
+    forward_y(6)
+    arrived(2)
+    take_q(2, other_rows)
+    kv_copy(0, other_rows).wait_recv()
+    kv_copy(1, mine_rows).wait_recv()
+    join_kv(mine_rows)
+    join_kv(other_rows)
+    for h in range(4):
+        attend(h, other_rows)
+
+    def out_copy(j):
+        return pltpu.make_async_remote_copy(
+            src_ref=sent.at[j], dst_ref=got.at[j], send_sem=o_send.at[j], recv_sem=o_recv.at[j],
+            device_id=x_dev, device_id_type=MESH,
+        )
+
+    def chip(i):
+        return block(i, 0) // 2
+
+    def columns(h, i):
+        return wob[h, :, pl.ds(pl.multiple_of(chip(i) * 256, 256), 256)]
+
+    def produce(h, start):
+        def step(i, carry):
+            for r in range(2):
+                to_core(6 + 2 * h + r, i, block(i, 1 - core)).wait_recv()
+            j = h * 8 + i
+            sent[j] = jnp.dot(
+                att[pl.ds(other_rows, ROWS), :], columns(h, i), preferred_element_type=jnp.float32
+            ).astype(jnp.bfloat16)
+            out_copy(j).start()
+            return carry
+
+        lax.fori_loop(start, start + 4, step, 0)
+
+    produce(0, 0)
+    forward_z(9)
+    forward_y(7)
+    produce(0, 4)
+    take_q(2, mine_rows)
+    forward_y(8)
+    produce(1, 0)
+    forward_y(9)
+    produce(1, 4)
+    for h in range(4):
+        attend(h, mine_rows)
+
+    def finish(j, carry):
+        h = j // 8
+        i = j % 8
+        kept = jnp.dot(
+            att[pl.ds(mine_rows, ROWS), :], columns(h, i), preferred_element_type=jnp.float32
+        ).astype(jnp.bfloat16)
+        out_copy(j).wait_recv()
+        total = (kept.astype(jnp.float32) + got[j].astype(jnp.float32)).astype(jnp.bfloat16)
+        base = chip(i) * 512 + h * 128
+        out[:, pl.ds(pl.multiple_of(base, 128), 128)] = total[:, :128]
+        out[:, pl.ds(pl.multiple_of(base + 256, 128), 128)] = total[:, 128:]
+        return carry
+
+    lax.fori_loop(0, 16, finish, 0)
+    for copy in sends:
+        copy.wait_send()
+    for condition, copy in maybe:
+        pl.when(condition)(copy.wait_send)
+
+    def drain(j, carry):
+        out_copy(j).wait_send()
+        return carry
+
+    lax.fori_loop(0, 16, drain, 0)
+
+
+def fused_body(tokens, wq, wq_s, wk, wk_s, wv, wv_s, wo, wo_s):
+    cosine, sine = rope_tables()
+    hbm = pl.BlockSpec(memory_space=pl.ANY)
+    dma = pltpu.SemaphoreType.DMA
+    bf16, f32 = jnp.bfloat16, jnp.float32
+    return pl.pallas_call(
+        fused_kernel,
+        out_shape=jax.ShapeDtypeStruct((ROWS, MODEL), bf16),
+        in_specs=[hbm] * 11,
+        out_specs=pl.BlockSpec(memory_space=pltpu.VMEM),
+        scratch_shapes=[
+            pltpu.VMEM((DEPTH, WIDTH), bf16),
+            pltpu.VMEM((64, DEPTH), bf16),
+            pltpu.VMEM((64, DEPTH), bf16),
+            pltpu.VMEM((WIDTH, DEPTH), bf16),
+            pltpu.VMEM((SPAN, HEAD), f32),
+            pltpu.VMEM((SPAN, HEAD), f32),
+            pltpu.SMEM((8, 32), f32),
+            pltpu.SMEM((1, 32), f32),
+            pltpu.SMEM((1, 32), f32),
+            pltpu.SMEM((8, 32), f32),
+            pltpu.VMEM((SPAN, MODEL), bf16),
+            pltpu.VMEM((2, MODEL, 256), bf16),
+            pltpu.VMEM((MODEL, 128), bf16),
+            pltpu.VMEM((2, WIDTH, MODEL // 2), bf16),
+            pltpu.VMEM((SPAN, HEAD), f32),
+            pltpu.VMEM((SPAN, HEAD), f32),
+            pltpu.VMEM((SPAN, 256), f32),
+            pltpu.VMEM((4, SPAN, HEAD), bf16),
+            pltpu.VMEM((SPAN, HEAD), bf16),
+            pltpu.VMEM((SPAN, HEAD), bf16),
+            pltpu.VMEM((SPAN, WIDTH), bf16),
+            pltpu.VMEM((16, ROWS, 256), bf16),
+            pltpu.VMEM((16, ROWS, 256), bf16),
+            dma((10, 5)), dma((10, 3)), dma((10, 4)), dma((10, 4)), dma((10, 8)), dma((10, 8)),
+            dma((TOKEN_PIECES,)), dma((TOKEN_PIECES,)), dma((11,)), dma((2,)), dma((2,)), dma((16,)), dma((16,)),
+        ],
+        compiler_params=pltpu.CompilerParams(
+            collective_id=0, has_side_effects=True, vmem_limit_bytes=VMEM_BYTES
+        ),
+        cost_estimate=pl.CostEstimate(flops=4_500_000_000, bytes_accessed=6_000_000, transcendentals=300_000),
+    )(tokens, wq, wq_s.T, wk.T, wk_s.T, wv.T, wv_s.T, wo, wo_s, jnp.asarray(cosine), jnp.asarray(sine))
+
+
 def solution(mesh):
+
+    fits = mesh.shape["dp"] == Z * Y * CORES and mesh.shape["tensor"] == 2
     return jax.shard_map(
-        body,
+        fused_body if fits else body,
         mesh=mesh,
         in_specs=(
             P(("dp", "tensor"), None),

time: 299 us -> 95.4 us (0.32)
  waiting for transfers between devices: 250 us -> 0 us
  Pallas kernels: 0 us -> 92.5 us
  matrix products: 23.7 us -> 0 us
  between operations: 13.7 us -> 0.01 us
  other arithmetic: 5.51 us -> 0 us
  starting transfers between devices: 5.3 us -> 0 us
    all_gather x5 -> x0, waiting for transfers between devices: 203 us -> none  [the longest x1 50.7 us: body(): wo_whole = lax.all_gather(wo_local, 'dp', axis=1, tiled=True)]
    pallas_call x0 -> x1, Pallas kernels: none -> 92.5 us  [fused_body(): pl.pallas_call(fused_kernel, out_shape=jax.ShapeDtypeStruct((ROWS, MODEL)...]
    reduce_scatter x1 -> x0, waiting for transfers between devices: 41.7 us -> none  [body(): lax.psum_scatter(terms.astype(jnp.bfloat16), 'tensor', scatter_dimension=...]
    dot_general x11 -> x0, matrix products: 23.7 us -> none  [the longest x1 5.72 us: body(): terms = jnp.dot(attended, wo_whole, preferred_element_type=jnp.float32)]
    ppermute x2 -> x0, starting transfers between devices: 5.09 us -> none  [from_partner(): return lax.ppermute(value, axis, pairs)]
    ppermute x2 -> x0, waiting for transfers between devices: 3.79 us -> none  [from_partner(): return lax.ppermute(value, axis, pairs)]
  transfers between devices with their start and end apart: 8 -> 0, of which waited for: 8 -> 0; matrix products, arithmetic and copies ran while one was open for 7% -> 0% of each run, Pallas kernels for 0% -> 0%
where the time goes in v2:
time: 95.4 us; the launch traced here: 95.2 us
  Pallas kernels  92.5 us (97%)
  local copies, waits for them, and re-layouts  2.7 us (3%)
    pallas_call x1, Pallas kernels, fused_body(): pl.pallas_call(fused_kernel, out_shape=jax.ShapeDtypeStruct((ROWS, MODEL)...  92.5 us
    unnamed x1, local copies, waits for them, and re-layouts  2.7 us

profile of v2, /device:TPU:0, one launch (start us, length us, event | category | flops | bytes accessed | tf_op | source)
XLA Modules:
  0.0 95.2 jit_solution(4369315182756111263)
XLA Ops:
  0.0 92.5 %shard_map.109 = bf16[192,4096]{1,0:T(8,128)(2,1)} custom-call(bf16[192,4096]{1,0:T(8,128)(2,1)} %tokens.1, bf16[256,512]{1,0:T(8,128)(2,1)} %wq_h.1, f32[8,32]{1,0:T(8,128)} %bitcast.7, bf16[64,256]{1,0:T(8,128)(2,1)} %bitcast.5, f32[1,32]{1,0:T(1,128)} %bitcast.8, bf16[64,256]{1,0:T(8,128)(2,1)} %bitcast.6, f32[1,32]{1,0:T(1,128)} %bitcast.9, ...), custom_call_target="tpu_custom_call" | custom-call | flops 4499999744 | bytes 6000000 | tf_op jit(solution)/shard_map/pallas_call | solution.py:470
  92.5 2.7 %copy.13 = bf16[192,4096]{1,0:T(8,128)(2,1)} copy(bf16[192,4096]{1,0:T(8,128)(2,1)} %shard_map.109) | data formatting | bytes 3145728
